TPU v7x, 32 devices: a whole 2x2x4 slice. The times are simulated.
32 devices in a mesh: horiz: 8 (over z, y), vert: 4 (over x, core).
Axes of the slice: x: 2, y: 2, z: 4, core: 2. Of those that a mesh axis runs over, the one named last changes fastest.
Arguments:
- tracer: bfloat16 [8, 2048, 128], P('vert', 'horiz'), may hold values from -6 to 6
- explicit_tiles: bfloat16 [8, 16, 7, 128, 128], P('vert', 'horiz'), may hold values from -0.25 to 0.25
- tile_columns: int32 [8, 16, 7], P('vert', 'horiz'), may hold values from 0 to 127, as said below
- tile_counts: int32 [8, 16], P('vert', 'horiz'), may hold values from 4 to 7
- surface_source: bfloat16 [2048, 128], P('horiz'), may hold values from -6 to 6
- implicit_columns: float32 [2048, 8, 8], P(('horiz', 'vert')), may hold values from -0.53033009 to 1
- settling: float32 [128], replicated, may hold values from 0.02 to 0.5
- wet_mask: int32 [8, 2048], P('vert', 'horiz'), may hold values 0 or 1
Outputs:
- tracer_out: bfloat16 [8, 2048, 128], P('vert', 'horiz')
Inputs may be any that keep to these rules, and one draw needn't show every extreme that they name: `tile_columns`: slot 0 of block row (l, t) names the row's own tile l * 16 + t; the other slots name distinct tiles within 2 levels and 2 tiles of it, inside the grid.
All inputs are finite; a program needn't handle non-finite values. No bound on the sum of `wet_mask` on one device may be relied on, other than what follows from the above.
Results may differ from a plain program's by a relative error of at most 0.015.
Values may be sent and summed in bfloat16 or wider, within the bound.
A program may use at most 64 MiB of HBM per device.

v0:
```python
import jax
import jax.numpy as jnp
from jax import lax
from jax.sharding import PartitionSpec as P

REACH = 2
STEPS = 4


def extended(shard, sides, width):
    for axis, dim in sides:
        size, length = (lax.axis_size(axis), shard.shape[dim])
        up = [(i, (i + 1) % size) for i in range(size - 1)]
        down = [(j, i) for i, j in up]
        last = lax.slice_in_dim(shard, length - width, length, axis=dim)
        leading = lax.slice_in_dim(shard, 0, width, axis=dim)
        before = lax.ppermute(last, axis, up)
        after = lax.ppermute(leading, axis, down)
        shard = jnp.concatenate([before, shard, after], axis=dim)
    return shard


def from_behind(value, axis, steps):
    count = lax.axis_size(axis)
    leading, last = (max(0, -steps), min(count, count - steps))
    return lax.ppermute(value, axis, [(source, source + steps) for source in range(leading, last)])


def on_device(
    tracer,
    explicit_tiles,
    tile_columns,
    tile_counts,
    surface_source,
    implicit_columns,
    settling,
    wet_mask,
):
    lev_dev, cells_dev, classes = tracer.shape
    tile_size = explicit_tiles.shape[-1]
    tiles_dev = cells_dev // tile_size
    slot_count = explicit_tiles.shape[2]
    h_tiles = tiles_dev * lax.axis_size("horiz")
    wide_tiles = tiles_dev + 2 * REACH
    first_level = lax.axis_index("vert") * lev_dev
    first_tile = lax.axis_index("horiz") * tiles_dev
    col_level = tile_columns // h_tiles - (first_level - REACH)
    col_tile = tile_columns % h_tiles - (first_tile - REACH)
    position = col_level * wide_tiles + col_tile
    live_slots = (
        jnp.arange(slot_count, dtype=jnp.int32)[None, None, :] < tile_counts[:, :, None]
    ).astype(jnp.bfloat16)
    on_top = first_level + jnp.arange(lev_dev, dtype=jnp.int32) == 0
    source = surface_source.astype(jnp.float32)
    fall_rate = settling[None, None, :]
    wet_cells = wet_mask.astype(jnp.bfloat16)[:, :, None]
    all_columns = lax.all_gather(implicit_columns, "vert", axis=0, tiled=True)
    own_rows = lax.dynamic_slice_in_dim(all_columns, first_level, lev_dev, 1)
    current = tracer
    for step_index in range(STEPS):
        slab_grid = current.reshape(lev_dev, tiles_dev, tile_size, classes)
        padded = extended(slab_grid, (("horiz", 1), ("vert", 0)), REACH)
        flattened = padded.reshape(-1, tile_size, classes)
        picked = flattened[position] * live_slots[:, :, :, None, None]
        explicit_flow = jnp.einsum(
            "ltjab,ltjbs->ltas", explicit_tiles, picked, preferred_element_type=jnp.float32
        )
        explicit_flow = explicit_flow.reshape(lev_dev, cells_dev, classes)
        explicit_flow = explicit_flow + jnp.where(on_top[:, None, None], source[None, :, :], 0.0)
        loaded = explicit_flow.astype(jnp.bfloat16)
        mixed_col = jnp.einsum(
            "ckm,mcs->kcs",
            own_rows,
            lax.all_gather(loaded, "vert", axis=0, tiled=True).astype(jnp.float32),
            precision=lax.Precision.HIGHEST,
        )
        upper_level = from_behind(mixed_col[-1].astype(jnp.bfloat16), "vert", 1).astype(jnp.float32)
        from_above = jnp.concatenate([upper_level[None], mixed_col[:-1]], axis=0)
        settled = (1.0 - fall_rate) * mixed_col + fall_rate * from_above
        current = (settled * wet_cells.astype(jnp.float32)).astype(jnp.bfloat16)
    return current


def solution(mesh):
    placed = (
        P("vert", "horiz", None),
        P("vert", "horiz", None, None, None),
        P("vert", "horiz", None),
        P("vert", "horiz"),
        P("horiz", None),
        P(("horiz", "vert"), None, None),
        P(),
        P("vert", "horiz"),
    )
    return jax.shard_map(
        on_device, mesh=mesh, in_specs=placed, out_specs=P("vert", "horiz", None), check_vma=False
    )
```

profile of v0, /device:TPU:1, one launch (start us, length us, event | category | flops | bytes accessed | tf_op | source)
XLA Modules:
  0.0 167.6 jit_solution(6005104641196930024)
XLA Ops:
  0.0 1.4 collective-permute-start.1
  1.4 4.6 %collective-permute-start = (bf16[2,2,128,128]{3,2,1,0:T(8,128)(2,1)}, bf16[2,2,128,128]{3,2,1,0:T(8,128)(2,1)S(1)}, u32[]{:S(2)}, u32[]{:S(2)}) collective-permute-start(bf16[2,2,128,128]{3,2,1,0:T(8,128)(2,1)} %bitcast.83), channel_id=1, source_target_pairs={{0,4},{4,8},{8,12},{12,16},{16,20},{20,24},{24,28},{1,5},{5,9},{9,... | collective-permute-start | bytes 393224 | tf_op jit(solution)/shard_map/ppermute | solution.py:17
  8.7 11.3 %all_gather.16 = f32[256,8,8]{2,1,0:T(8,128)S(1)} all-gather(f32[64,8,8]{2,1,0:T(8,128)S(1)} %copy.38), channel_id=1, replica_groups=mesh['horiz'=8,'vert'=4] {'vert'}, dimensions={0}, use_global_device_ids=true | all-gather | bytes 81920 | tf_op jit(solution)/shard_map/all_gather | solution.py:57
  20.1 2.1 %collective-permute-start.3 = (bf16[2,6,128,128]{3,2,1,0:T(8,128)(2,1)S(1)}, bf16[2,6,128,128]{3,2,1,0:T(8,128)(2,1)S(1)}, u32[]{:S(2)}, u32[]{:S(2)}) collective-permute-start(bf16[2,6,128,128]{3,2,1,0:T(8,128)(2,1)S(1)} %pad_maximum_fusion.4), channel_id=1, source_target_pairs={{1,0},{2,1},{3,2},{5,4},{6,5},{7,6},{9,8},{10,9},{11,10},{13,12},{... | collective-permute-start | bytes 1179656 | tf_op jit(solution)/shard_map/ppermute | solution.py:18
  22.1 3.5 %collective-permute-start.2 = (bf16[2,6,128,128]{3,2,1,0:T(8,128)(2,1)S(1)}, bf16[2,6,128,128]{3,2,1,0:T(8,128)(2,1)S(1)}, u32[]{:S(2)}, u32[]{:S(2)}) collective-permute-start(bf16[2,6,128,128]{3,2,1,0:T(8,128)(2,1)S(1)} %pad_maximum_fusion.4), channel_id=1, source_target_pairs={{0,1},{1,2},{2,3},{4,5},{5,6},{6,7},{8,9},{9,10},{10,11},{12,13},{... | collective-permute-start | bytes 1179656 | tf_op jit(solution)/shard_map/ppermute | solution.py:17
  25.7 3.4 %collective-permute-done.3 = bf16[2,6,128,128]{3,2,1,0:T(8,128)(2,1)S(1)} collective-permute-done((bf16[2,6,128,128]{3,2,1,0:T(8,128)(2,1)S(1)}, bf16[2,6,128,128]{3,2,1,0:T(8,128)(2,1)S(1)}, u32[]{:S(2)}, u32[]{:S(2)}) %collective-permute-start.3) | collective-permute-done | bytes 393248 | tf_op jit(solution)/shard_map/ppermute | solution.py:18
  31.4 1.6 gather_fusion
  33.0 1.7 fusion.6
  34.8 8.4 %all_gather.15 = bf16[8,256,128]{2,1,0:T(8,128)(2,1)S(1)} all-gather(bf16[2,256,128]{2,1,0:T(8,128)(2,1)S(1)} %fusion.16), channel_id=1, replica_groups=mesh['horiz'=8,'vert'=4] {'vert'}, dimensions={0}, use_global_device_ids=true | all-gather | bytes 655360 | tf_op jit(solution)/shard_map/all_gather | solution.py:74
  44.6 2.5 %collective-permute-start.4 = (bf16[256,128]{1,0:T(8,128)(2,1)S(1)}, bf16[256,128]{1,0:T(8,128)(2,1)S(1)}, u32[]{:S(2)}, u32[]{:S(2)}) collective-permute-start(bf16[256,128]{1,0:T(8,128)(2,1)S(1)} %bitcast.90), channel_id=1, source_target_pairs={{0,1},{1,2},{2,3},{4,5},{5,6},{6,7},{8,9},{9,10},{10,11},{12,13},{... | collective-permute-start | bytes 196616 | tf_op jit(solution)/shard_map/ppermute | solution.py:26
  48.8 4.0 %collective-permute-start.5 = (bf16[2,2,128,128]{3,2,1,0:T(8,128)(2,1)S(1)}, bf16[2,2,128,128]{3,2,1,0:T(8,128)(2,1)S(1)}, u32[]{:S(2)}, u32[]{:S(2)}) collective-permute-start(bf16[2,2,128,128]{3,2,1,0:T(8,128)(2,1)S(1)} %copy.42), channel_id=1, source_target_pairs={{0,4},{4,8},{8,12},{12,16},{16,20},{20,24},{24,28},{1,5},{5,9},{9,... | collective-permute-start | bytes 393224 | tf_op jit(solution)/shard_map/ppermute | solution.py:17
  52.9 1.3 collective-permute-start.6
  54.2 2.0 %collective-permute-done.5 = bf16[2,2,128,128]{3,2,1,0:T(8,128)(2,1)S(1)} collective-permute-done((bf16[2,2,128,128]{3,2,1,0:T(8,128)(2,1)S(1)}, bf16[2,2,128,128]{3,2,1,0:T(8,128)(2,1)S(1)}, u32[]{:S(2)}, u32[]{:S(2)}) %collective-permute-start.5) | collective-permute-done | bytes 131104 | tf_op jit(solution)/shard_map/ppermute | solution.py:17
  56.2 3.8 %collective-permute-done.6 = bf16[2,2,128,128]{3,2,1,0:T(8,128)(2,1)S(1)} collective-permute-done((bf16[2,2,128,128]{3,2,1,0:T(8,128)(2,1)S(1)}, bf16[2,2,128,128]{3,2,1,0:T(8,128)(2,1)S(1)}, u32[]{:S(2)}, u32[]{:S(2)}) %collective-permute-start.6) | collective-permute-done | bytes 131104 | tf_op jit(solution)/shard_map/ppermute | solution.py:18
  60.1 2.5 %collective-permute-start.8 = (bf16[2,6,128,128]{3,2,1,0:T(8,128)(2,1)S(1)}, bf16[2,6,128,128]{3,2,1,0:T(8,128)(2,1)S(1)}, u32[]{:S(2)}, u32[]{:S(2)}) collective-permute-start(bf16[2,6,128,128]{3,2,1,0:T(8,128)(2,1)S(1)} %constant_dynamic-update-slice_fusion), channel_id=1, source_target_pairs={{1,0},{2,1},{3,2},{5,4},{6,5},{7,6},{9,8},{10,9},{11,10},{13,12},{... | collective-permute-start | bytes 1179656 | tf_op jit(solution)/shard_map/ppermute | solution.py:18
  62.6 3.6 %collective-permute-start.7 = (bf16[2,6,128,128]{3,2,1,0:T(8,128)(2,1)S(1)}, bf16[2,6,128,128]{3,2,1,0:T(8,128)(2,1)S(1)}, u32[]{:S(2)}, u32[]{:S(2)}) collective-permute-start(bf16[2,6,128,128]{3,2,1,0:T(8,128)(2,1)S(1)} %constant_dynamic-update-slice_fusion), channel_id=1, source_target_pairs={{0,1},{1,2},{2,3},{4,5},{5,6},{6,7},{8,9},{9,10},{10,11},{12,13},{... | collective-permute-start | bytes 1179656 | tf_op jit(solution)/shard_map/ppermute | solution.py:17
  66.2 3.5 %collective-permute-done.8 = bf16[2,6,128,128]{3,2,1,0:T(8,128)(2,1)S(1)} collective-permute-done((bf16[2,6,128,128]{3,2,1,0:T(8,128)(2,1)S(1)}, bf16[2,6,128,128]{3,2,1,0:T(8,128)(2,1)S(1)}, u32[]{:S(2)}, u32[]{:S(2)}) %collective-permute-start.8) | collective-permute-done | bytes 393248 | tf_op jit(solution)/shard_map/ppermute | solution.py:18
  71.1 1.6 gather_fusion.1
  72.7 1.6 fusion.4
  74.5 8.4 %all_gather.17 = bf16[8,256,128]{2,1,0:T(8,128)(2,1)S(1)} all-gather(bf16[2,256,128]{2,1,0:T(8,128)(2,1)S(1)} %fusion.17), channel_id=1, replica_groups=mesh['horiz'=8,'vert'=4] {'vert'}, dimensions={0}, use_global_device_ids=true | all-gather | bytes 655360 | tf_op jit(solution)/shard_map/all_gather | solution.py:74
  84.2 2.5 %collective-permute-start.9 = (bf16[256,128]{1,0:T(8,128)(2,1)S(1)}, bf16[256,128]{1,0:T(8,128)(2,1)S(1)}, u32[]{:S(2)}, u32[]{:S(2)}) collective-permute-start(bf16[256,128]{1,0:T(8,128)(2,1)S(1)} %bitcast.91), channel_id=1, source_target_pairs={{0,1},{1,2},{2,3},{4,5},{5,6},{6,7},{8,9},{9,10},{10,11},{12,13},{... | collective-permute-start | bytes 196616 | tf_op jit(solution)/shard_map/ppermute | solution.py:26
  86.8 1.2 collective-permute-done.9
  88.5 3.1 %collective-permute-start.10 = (bf16[2,2,128,128]{3,2,1,0:T(8,128)(2,1)S(1)}, bf16[2,2,128,128]{3,2,1,0:T(8,128)(2,1)S(1)}, u32[]{:S(2)}, u32[]{:S(2)}) collective-permute-start(bf16[2,2,128,128]{3,2,1,0:T(8,128)(2,1)S(1)} %copy.47), channel_id=1, source_target_pairs={{0,4},{4,8},{8,12},{12,16},{16,20},{20,24},{24,28},{1,5},{5,9},{9,... | collective-permute-start | bytes 393224 | tf_op jit(solution)/shard_map/ppermute | solution.py:17
  91.6 1.3 collective-permute-start.11
  92.9 2.0 %collective-permute-done.10 = bf16[2,2,128,128]{3,2,1,0:T(8,128)(2,1)S(1)} collective-permute-done((bf16[2,2,128,128]{3,2,1,0:T(8,128)(2,1)S(1)}, bf16[2,2,128,128]{3,2,1,0:T(8,128)(2,1)S(1)}, u32[]{:S(2)}, u32[]{:S(2)}) %collective-permute-start.10) | collective-permute-done | bytes 131104 | tf_op jit(solution)/shard_map/ppermute | solution.py:17
  95.0 3.8 %collective-permute-done.11 = bf16[2,2,128,128]{3,2,1,0:T(8,128)(2,1)S(1)} collective-permute-done((bf16[2,2,128,128]{3,2,1,0:T(8,128)(2,1)S(1)}, bf16[2,2,128,128]{3,2,1,0:T(8,128)(2,1)S(1)}, u32[]{:S(2)}, u32[]{:S(2)}) %collective-permute-start.11) | collective-permute-done | bytes 131104 | tf_op jit(solution)/shard_map/ppermute | solution.py:18
  98.8 2.5 %collective-permute-start.13 = (bf16[2,6,128,128]{3,2,1,0:T(8,128)(2,1)S(1)}, bf16[2,6,128,128]{3,2,1,0:T(8,128)(2,1)S(1)}, u32[]{:S(2)}, u32[]{:S(2)}) collective-permute-start(bf16[2,6,128,128]{3,2,1,0:T(8,128)(2,1)S(1)} %constant_dynamic-update-slice_fusion.3), channel_id=1, source_target_pairs={{1,0},{2,1},{3,2},{5,4},{6,5},{7,6},{9,8},{10,9},{11,10},{13,12},{... | collective-permute-start | bytes 1179656 | tf_op jit(solution)/shard_map/ppermute | solution.py:18
  101.4 3.6 %collective-permute-start.12 = (bf16[2,6,128,128]{3,2,1,0:T(8,128)(2,1)S(1)}, bf16[2,6,128,128]{3,2,1,0:T(8,128)(2,1)S(1)}, u32[]{:S(2)}, u32[]{:S(2)}) collective-permute-start(bf16[2,6,128,128]{3,2,1,0:T(8,128)(2,1)S(1)} %constant_dynamic-update-slice_fusion.3), channel_id=1, source_target_pairs={{0,1},{1,2},{2,3},{4,5},{5,6},{6,7},{8,9},{9,10},{10,11},{12,13},{... | collective-permute-start | bytes 1179656 | tf_op jit(solution)/shard_map/ppermute | solution.py:17
  105.0 3.5 %collective-permute-done.13 = bf16[2,6,128,128]{3,2,1,0:T(8,128)(2,1)S(1)} collective-permute-done((bf16[2,6,128,128]{3,2,1,0:T(8,128)(2,1)S(1)}, bf16[2,6,128,128]{3,2,1,0:T(8,128)(2,1)S(1)}, u32[]{:S(2)}, u32[]{:S(2)}) %collective-permute-start.13) | collective-permute-done | bytes 393248 | tf_op jit(solution)/shard_map/ppermute | solution.py:18
  109.8 1.6 gather_fusion.2
  111.5 1.7 fusion.2
  113.2 8.4 %all_gather.18 = bf16[8,256,128]{2,1,0:T(8,128)(2,1)S(1)} all-gather(bf16[2,256,128]{2,1,0:T(8,128)(2,1)S(1)} %fusion.18), channel_id=1, replica_groups=mesh['horiz'=8,'vert'=4] {'vert'}, dimensions={0}, use_global_device_ids=true | all-gather | bytes 655360 | tf_op jit(solution)/shard_map/all_gather | solution.py:74
  121.6 1.2 convolution_bitcast_fusion.1
  123.0 2.5 %collective-permute-start.14 = (bf16[256,128]{1,0:T(8,128)(2,1)S(1)}, bf16[256,128]{1,0:T(8,128)(2,1)S(1)}, u32[]{:S(2)}, u32[]{:S(2)}) collective-permute-start(bf16[256,128]{1,0:T(8,128)(2,1)S(1)} %bitcast.92), channel_id=1, source_target_pairs={{0,1},{1,2},{2,3},{4,5},{5,6},{6,7},{8,9},{9,10},{10,11},{12,13},{... | collective-permute-start | bytes 196616 | tf_op jit(solution)/shard_map/ppermute | solution.py:26
  125.6 1.2 collective-permute-done.14
  127.2 4.1 %collective-permute-start.15 = (bf16[2,2,128,128]{3,2,1,0:T(8,128)(2,1)S(1)}, bf16[2,2,128,128]{3,2,1,0:T(8,128)(2,1)S(1)}, u32[]{:S(2)}, u32[]{:S(2)}) collective-permute-start(bf16[2,2,128,128]{3,2,1,0:T(8,128)(2,1)S(1)} %copy.51), channel_id=1, source_target_pairs={{0,4},{4,8},{8,12},{12,16},{16,20},{20,24},{24,28},{1,5},{5,9},{9,... | collective-permute-start | bytes 393224 | tf_op jit(solution)/shard_map/ppermute | solution.py:17
  131.3 1.3 collective-permute-start.16
  132.6 2.0 %collective-permute-done.15 = bf16[2,2,128,128]{3,2,1,0:T(8,128)(2,1)S(1)} collective-permute-done((bf16[2,2,128,128]{3,2,1,0:T(8,128)(2,1)S(1)}, bf16[2,2,128,128]{3,2,1,0:T(8,128)(2,1)S(1)}, u32[]{:S(2)}, u32[]{:S(2)}) %collective-permute-start.15) | collective-permute-done | bytes 131104 | tf_op jit(solution)/shard_map/ppermute | solution.py:17
  134.6 3.8 %collective-permute-done.16 = bf16[2,2,128,128]{3,2,1,0:T(8,128)(2,1)S(1)} collective-permute-done((bf16[2,2,128,128]{3,2,1,0:T(8,128)(2,1)S(1)}, bf16[2,2,128,128]{3,2,1,0:T(8,128)(2,1)S(1)}, u32[]{:S(2)}, u32[]{:S(2)}) %collective-permute-start.16) | collective-permute-done | bytes 131104 | tf_op jit(solution)/shard_map/ppermute | solution.py:18
  138.5 2.5 %collective-permute-start.18 = (bf16[2,6,128,128]{3,2,1,0:T(8,128)(2,1)S(1)}, bf16[2,6,128,128]{3,2,1,0:T(8,128)(2,1)S(1)}, u32[]{:S(2)}, u32[]{:S(2)}) collective-permute-start(bf16[2,6,128,128]{3,2,1,0:T(8,128)(2,1)S(1)} %constant_dynamic-update-slice_fusion.6), channel_id=1, source_target_pairs={{1,0},{2,1},{3,2},{5,4},{6,5},{7,6},{9,8},{10,9},{11,10},{13,12},{... | collective-permute-start | bytes 1179656 | tf_op jit(solution)/shard_map/ppermute | solution.py:18
  141.0 3.8 %collective-permute-start.17 = (bf16[2,6,128,128]{3,2,1,0:T(8,128)(2,1)S(1)}, bf16[2,6,128,128]{3,2,1,0:T(8,128)(2,1)S(1)}, u32[]{:S(2)}, u32[]{:S(2)}) collective-permute-start(bf16[2,6,128,128]{3,2,1,0:T(8,128)(2,1)S(1)} %constant_dynamic-update-slice_fusion.6), channel_id=1, source_target_pairs={{0,1},{1,2},{2,3},{4,5},{5,6},{6,7},{8,9},{9,10},{10,11},{12,13},{... | collective-permute-start | bytes 1179656 | tf_op jit(solution)/shard_map/ppermute | solution.py:17
  144.9 3.3 %collective-permute-done.18 = bf16[2,6,128,128]{3,2,1,0:T(8,128)(2,1)S(1)} collective-permute-done((bf16[2,6,128,128]{3,2,1,0:T(8,128)(2,1)S(1)}, bf16[2,6,128,128]{3,2,1,0:T(8,128)(2,1)S(1)}, u32[]{:S(2)}, u32[]{:S(2)}) %collective-permute-start.18) | collective-permute-done | bytes 393248 | tf_op jit(solution)/shard_map/ppermute | solution.py:18
  149.5 1.6 gather_fusion.3
  151.1 1.6 fusion
  152.9 8.4 %all_gather.19 = bf16[8,256,128]{2,1,0:T(8,128)(2,1)S(1)} all-gather(bf16[2,256,128]{2,1,0:T(8,128)(2,1)S(1)} %fusion.19), channel_id=1, replica_groups=mesh['horiz'=8,'vert'=4] {'vert'}, dimensions={0}, use_global_device_ids=true | all-gather | bytes 655360 | tf_op jit(solution)/shard_map/all_gather | solution.py:74
  161.3 1.2 convolution_bitcast_fusion
  162.7 2.5 %collective-permute-start.19 = (bf16[256,128]{1,0:T(8,128)(2,1)S(1)}, bf16[256,128]{1,0:T(8,128)(2,1)S(1)}, u32[]{:S(2)}, u32[]{:S(2)}) collective-permute-start(bf16[256,128]{1,0:T(8,128)(2,1)S(1)} %bitcast.93), channel_id=1, source_target_pairs={{0,1},{1,2},{2,3},{4,5},{5,6},{6,7},{8,9},{9,10},{10,11},{12,13},{... | collective-permute-start | bytes 196616 | tf_op jit(solution)/shard_map/ppermute | solution.py:26
  165.3 1.2 collective-permute-done.19
  (73 shorter events, 16.3 us)
Async XLA Ops:
  0.0 33.0 %copy-start = (bf16[2,2,7,128,128]{4,3,2,1,0:T(8,128)(2,1)S(1)}, bf16[2,2,7,128,128]{4,3,2,1,0:T(8,128)(2,1)}, u32[]{:S(2)}) copy-start(bf16[2,2,7,128,128]{4,3,2,1,0:T(8,128)(2,1)} %param.9) | copy-start | bytes 2752516
  0.0 20.0 %copy-start.1 = (bf16[2,256,128]{2,1,0:T(8,128)(2,1)S(1)}, bf16[2,256,128]{2,1,0:T(8,128)(2,1)}, u32[]{:S(2)}) copy-start(bf16[2,256,128]{2,1,0:T(8,128)(2,1)} %param.8) | copy-start | bytes 393220
  0.0 20.0 %collective-permute-start.1 = (bf16[2,2,128,128]{3,2,1,0:T(8,128)(2,1)}, bf16[2,2,128,128]{3,2,1,0:T(8,128)(2,1)S(1)}, u32[]{:S(2)}, u32[]{:S(2)}) collective-permute-start(bf16[2,2,128,128]{3,2,1,0:T(8,128)(2,1)} %bitcast.82), channel_id=1, source_target_pairs={{4,0},{8,4},{12,8},{16,12},{20,16},{24,20},{28,24},{5,1},{9,5},{13... | collective-permute-start | bytes 393224 | tf_op jit(solution)/shard_map/ppermute | solution.py:18
  1.4 18.6 %collective-permute-start = (bf16[2,2,128,128]{3,2,1,0:T(8,128)(2,1)}, bf16[2,2,128,128]{3,2,1,0:T(8,128)(2,1)S(1)}, u32[]{:S(2)}, u32[]{:S(2)}) collective-permute-start(bf16[2,2,128,128]{3,2,1,0:T(8,128)(2,1)} %bitcast.83), channel_id=1, source_target_pairs={{0,4},{4,8},{8,12},{12,16},{16,20},{20,24},{24,28},{1,5},{5,9},{9,... | collective-permute-start | bytes 393224 | tf_op jit(solution)/shard_map/ppermute | solution.py:17
  7.7 17.9 %copy-start.5 = (s32[2,2]{1,0:T(2,128)S(1)}, s32[2,2]{1,0:T(2,128)}, u32[]{:S(2)}) copy-start(s32[2,2]{1,0:T(2,128)} %param.11) | copy-start | bytes 52
  7.7 18.0 %copy-start.4 = (s32[2,256]{1,0:T(2,128)S(1)}, s32[2,256]{1,0:T(2,128)}, u32[]{:S(2)}) copy-start(s32[2,256]{1,0:T(2,128)} %param.15) | copy-start | bytes 6148
  20.0 9.2 %copy-start.2 = (bf16[2,2,128,128]{3,2,1,0:T(8,128)(2,1)}, bf16[2,2,128,128]{3,2,1,0:T(8,128)(2,1)S(1)}, u32[]{:S(2)}) copy-start(bf16[2,2,128,128]{3,2,1,0:T(8,128)(2,1)S(1)} %collective-permute-done) | copy-start | bytes 393220
  20.1 9.1 %collective-permute-start.3 = (bf16[2,6,128,128]{3,2,1,0:T(8,128)(2,1)S(1)}, bf16[2,6,128,128]{3,2,1,0:T(8,128)(2,1)S(1)}, u32[]{:S(2)}, u32[]{:S(2)}) collective-permute-start(bf16[2,6,128,128]{3,2,1,0:T(8,128)(2,1)S(1)} %pad_maximum_fusion.4), channel_id=1, source_target_pairs={{1,0},{2,1},{3,2},{5,4},{6,5},{7,6},{9,8},{10,9},{11,10},{13,12},{... | collective-permute-start | bytes 1179656 | tf_op jit(solution)/shard_map/ppermute | solution.py:18
  22.1 8.2 %collective-permute-start.2 = (bf16[2,6,128,128]{3,2,1,0:T(8,128)(2,1)S(1)}, bf16[2,6,128,128]{3,2,1,0:T(8,128)(2,1)S(1)}, u32[]{:S(2)}, u32[]{:S(2)}) collective-permute-start(bf16[2,6,128,128]{3,2,1,0:T(8,128)(2,1)S(1)} %pad_maximum_fusion.4), channel_id=1, source_target_pairs={{0,1},{1,2},{2,3},{4,5},{5,6},{6,7},{8,9},{9,10},{10,11},{12,13},{... | collective-permute-start | bytes 1179656 | tf_op jit(solution)/shard_map/ppermute | solution.py:17
  34.8 12.3 %copy-start.3 = (f32[128]{0:T(128)S(1)}, f32[128]{0:T(128)}, u32[]{:S(2)}) copy-start(f32[128]{0:T(128)} %param.14) | copy-start | bytes 1540
  44.6 3.8 %collective-permute-start.4 = (bf16[256,128]{1,0:T(8,128)(2,1)S(1)}, bf16[256,128]{1,0:T(8,128)(2,1)S(1)}, u32[]{:S(2)}, u32[]{:S(2)}) collective-permute-start(bf16[256,128]{1,0:T(8,128)(2,1)S(1)} %bitcast.90), channel_id=1, source_target_pairs={{0,1},{1,2},{2,3},{4,5},{5,6},{6,7},{8,9},{9,10},{10,11},{12,13},{... | collective-permute-start | bytes 196616 | tf_op jit(solution)/shard_map/ppermute | solution.py:26
  48.8 7.3 %collective-permute-start.5 = (bf16[2,2,128,128]{3,2,1,0:T(8,128)(2,1)S(1)}, bf16[2,2,128,128]{3,2,1,0:T(8,128)(2,1)S(1)}, u32[]{:S(2)}, u32[]{:S(2)}) collective-permute-start(bf16[2,2,128,128]{3,2,1,0:T(8,128)(2,1)S(1)} %copy.42), channel_id=1, source_target_pairs={{0,4},{4,8},{8,12},{12,16},{16,20},{20,24},{24,28},{1,5},{5,9},{9,... | collective-permute-start | bytes 393224 | tf_op jit(solution)/shard_map/ppermute | solution.py:17
  52.9 7.2 %collective-permute-start.6 = (bf16[2,2,128,128]{3,2,1,0:T(8,128)(2,1)S(1)}, bf16[2,2,128,128]{3,2,1,0:T(8,128)(2,1)S(1)}, u32[]{:S(2)}, u32[]{:S(2)}) collective-permute-start(bf16[2,2,128,128]{3,2,1,0:T(8,128)(2,1)S(1)} %copy.42), channel_id=1, source_target_pairs={{4,0},{8,4},{12,8},{16,12},{20,16},{24,20},{28,24},{5,1},{9,5},{13... | collective-permute-start | bytes 393224 | tf_op jit(solution)/shard_map/ppermute | solution.py:18
  60.1 9.7 %collective-permute-start.8 = (bf16[2,6,128,128]{3,2,1,0:T(8,128)(2,1)S(1)}, bf16[2,6,128,128]{3,2,1,0:T(8,128)(2,1)S(1)}, u32[]{:S(2)}, u32[]{:S(2)}) collective-permute-start(bf16[2,6,128,128]{3,2,1,0:T(8,128)(2,1)S(1)} %constant_dynamic-update-slice_fusion), channel_id=1, source_target_pairs={{1,0},{2,1},{3,2},{5,4},{6,5},{7,6},{9,8},{10,9},{11,10},{13,12},{... | collective-permute-start | bytes 1179656 | tf_op jit(solution)/shard_map/ppermute | solution.py:18
  62.6 8.3 %collective-permute-start.7 = (bf16[2,6,128,128]{3,2,1,0:T(8,128)(2,1)S(1)}, bf16[2,6,128,128]{3,2,1,0:T(8,128)(2,1)S(1)}, u32[]{:S(2)}, u32[]{:S(2)}) collective-permute-start(bf16[2,6,128,128]{3,2,1,0:T(8,128)(2,1)S(1)} %constant_dynamic-update-slice_fusion), channel_id=1, source_target_pairs={{0,1},{1,2},{2,3},{4,5},{5,6},{6,7},{8,9},{9,10},{10,11},{12,13},{... | collective-permute-start | bytes 1179656 | tf_op jit(solution)/shard_map/ppermute | solution.py:17
  84.2 3.8 %collective-permute-start.9 = (bf16[256,128]{1,0:T(8,128)(2,1)S(1)}, bf16[256,128]{1,0:T(8,128)(2,1)S(1)}, u32[]{:S(2)}, u32[]{:S(2)}) collective-permute-start(bf16[256,128]{1,0:T(8,128)(2,1)S(1)} %bitcast.91), channel_id=1, source_target_pairs={{0,1},{1,2},{2,3},{4,5},{5,6},{6,7},{8,9},{9,10},{10,11},{12,13},{... | collective-permute-start | bytes 196616 | tf_op jit(solution)/shard_map/ppermute | solution.py:26
  88.5 6.4 %collective-permute-start.10 = (bf16[2,2,128,128]{3,2,1,0:T(8,128)(2,1)S(1)}, bf16[2,2,128,128]{3,2,1,0:T(8,128)(2,1)S(1)}, u32[]{:S(2)}, u32[]{:S(2)}) collective-permute-start(bf16[2,2,128,128]{3,2,1,0:T(8,128)(2,1)S(1)} %copy.47), channel_id=1, source_target_pairs={{0,4},{4,8},{8,12},{12,16},{16,20},{20,24},{24,28},{1,5},{5,9},{9,... | collective-permute-start | bytes 393224 | tf_op jit(solution)/shard_map/ppermute | solution.py:17
  91.6 7.2 %collective-permute-start.11 = (bf16[2,2,128,128]{3,2,1,0:T(8,128)(2,1)S(1)}, bf16[2,2,128,128]{3,2,1,0:T(8,128)(2,1)S(1)}, u32[]{:S(2)}, u32[]{:S(2)}) collective-permute-start(bf16[2,2,128,128]{3,2,1,0:T(8,128)(2,1)S(1)} %copy.47), channel_id=1, source_target_pairs={{4,0},{8,4},{12,8},{16,12},{20,16},{24,20},{28,24},{5,1},{9,5},{13... | collective-permute-start | bytes 393224 | tf_op jit(solution)/shard_map/ppermute | solution.py:18
  98.8 9.7 %collective-permute-start.13 = (bf16[2,6,128,128]{3,2,1,0:T(8,128)(2,1)S(1)}, bf16[2,6,128,128]{3,2,1,0:T(8,128)(2,1)S(1)}, u32[]{:S(2)}, u32[]{:S(2)}) collective-permute-start(bf16[2,6,128,128]{3,2,1,0:T(8,128)(2,1)S(1)} %constant_dynamic-update-slice_fusion.3), channel_id=1, source_target_pairs={{1,0},{2,1},{3,2},{5,4},{6,5},{7,6},{9,8},{10,9},{11,10},{13,12},{... | collective-permute-start | bytes 1179656 | tf_op jit(solution)/shard_map/ppermute | solution.py:18
  101.4 8.3 %collective-permute-start.12 = (bf16[2,6,128,128]{3,2,1,0:T(8,128)(2,1)S(1)}, bf16[2,6,128,128]{3,2,1,0:T(8,128)(2,1)S(1)}, u32[]{:S(2)}, u32[]{:S(2)}) collective-permute-start(bf16[2,6,128,128]{3,2,1,0:T(8,128)(2,1)S(1)} %constant_dynamic-update-slice_fusion.3), channel_id=1, source_target_pairs={{0,1},{1,2},{2,3},{4,5},{5,6},{6,7},{8,9},{9,10},{10,11},{12,13},{... | collective-permute-start | bytes 1179656 | tf_op jit(solution)/shard_map/ppermute | solution.py:17
  123.0 3.8 %collective-permute-start.14 = (bf16[256,128]{1,0:T(8,128)(2,1)S(1)}, bf16[256,128]{1,0:T(8,128)(2,1)S(1)}, u32[]{:S(2)}, u32[]{:S(2)}) collective-permute-start(bf16[256,128]{1,0:T(8,128)(2,1)S(1)} %bitcast.92), channel_id=1, source_target_pairs={{0,1},{1,2},{2,3},{4,5},{5,6},{6,7},{8,9},{9,10},{10,11},{12,13},{... | collective-permute-start | bytes 196616 | tf_op jit(solution)/shard_map/ppermute | solution.py:26
  127.2 7.3 %collective-permute-start.15 = (bf16[2,2,128,128]{3,2,1,0:T(8,128)(2,1)S(1)}, bf16[2,2,128,128]{3,2,1,0:T(8,128)(2,1)S(1)}, u32[]{:S(2)}, u32[]{:S(2)}) collective-permute-start(bf16[2,2,128,128]{3,2,1,0:T(8,128)(2,1)S(1)} %copy.51), channel_id=1, source_target_pairs={{0,4},{4,8},{8,12},{12,16},{16,20},{20,24},{24,28},{1,5},{5,9},{9,... | collective-permute-start | bytes 393224 | tf_op jit(solution)/shard_map/ppermute | solution.py:17
  131.3 7.2 %collective-permute-start.16 = (bf16[2,2,128,128]{3,2,1,0:T(8,128)(2,1)S(1)}, bf16[2,2,128,128]{3,2,1,0:T(8,128)(2,1)S(1)}, u32[]{:S(2)}, u32[]{:S(2)}) collective-permute-start(bf16[2,2,128,128]{3,2,1,0:T(8,128)(2,1)S(1)} %copy.51), channel_id=1, source_target_pairs={{4,0},{8,4},{12,8},{16,12},{20,16},{24,20},{28,24},{5,1},{9,5},{13... | collective-permute-start | bytes 393224 | tf_op jit(solution)/shard_map/ppermute | solution.py:18
  138.5 9.7 %collective-permute-start.18 = (bf16[2,6,128,128]{3,2,1,0:T(8,128)(2,1)S(1)}, bf16[2,6,128,128]{3,2,1,0:T(8,128)(2,1)S(1)}, u32[]{:S(2)}, u32[]{:S(2)}) collective-permute-start(bf16[2,6,128,128]{3,2,1,0:T(8,128)(2,1)S(1)} %constant_dynamic-update-slice_fusion.6), channel_id=1, source_target_pairs={{1,0},{2,1},{3,2},{5,4},{6,5},{7,6},{9,8},{10,9},{11,10},{13,12},{... | collective-permute-start | bytes 1179656 | tf_op jit(solution)/shard_map/ppermute | solution.py:18
  141.0 8.3 %collective-permute-start.17 = (bf16[2,6,128,128]{3,2,1,0:T(8,128)(2,1)S(1)}, bf16[2,6,128,128]{3,2,1,0:T(8,128)(2,1)S(1)}, u32[]{:S(2)}, u32[]{:S(2)}) collective-permute-start(bf16[2,6,128,128]{3,2,1,0:T(8,128)(2,1)S(1)} %constant_dynamic-update-slice_fusion.6), channel_id=1, source_target_pairs={{0,1},{1,2},{2,3},{4,5},{5,6},{6,7},{8,9},{9,10},{10,11},{12,13},{... | collective-permute-start | bytes 1179656 | tf_op jit(solution)/shard_map/ppermute | solution.py:17
  162.7 3.8 %collective-permute-start.19 = (bf16[256,128]{1,0:T(8,128)(2,1)S(1)}, bf16[256,128]{1,0:T(8,128)(2,1)S(1)}, u32[]{:S(2)}, u32[]{:S(2)}) collective-permute-start(bf16[256,128]{1,0:T(8,128)(2,1)S(1)} %bitcast.93), channel_id=1, source_target_pairs={{0,1},{1,2},{2,3},{4,5},{5,6},{6,7},{8,9},{9,10},{10,11},{12,13},{... | collective-permute-start | bytes 196616 | tf_op jit(solution)/shard_map/ppermute | solution.py:26
where the time goes:
time: 169 us; the launch traced here: 168 us
  starting transfers between devices  55.3 us (33%)
  blocking collectives  44.9 us (27%)
  waiting for transfers between devices  40.7 us (24%)
  matrix products  11.4 us (7%)
  local copies, waits for them, and re-layouts  9.57 us (6%)
  other arithmetic  5.1 us (3%)
    all_gather x4, blocking collectives, on_device(): lax.all_gather(loaded, 'vert', axis=0, tiled=True).astype(jnp.float32)  33.6 us
    ppermute x8, starting transfers between devices, extended(): before = lax.ppermute(last, axis, up)  30.4 us
    ppermute x8, waiting for transfers between devices, extended(): after = lax.ppermute(leading, axis, down)  25.3 us
    ppermute x8, starting transfers between devices, extended(): after = lax.ppermute(leading, axis, down)  14.9 us
    all_gather x1, blocking collectives, on_device(): all_columns = lax.all_gather(implicit_columns, 'vert', axis=0, tiled=True)  11.3 us
    ppermute x8, waiting for transfers between devices, extended(): before = lax.ppermute(last, axis, up)  10.7 us
    ppermute x4, starting transfers between devices, from_behind(): lax.ppermute(value, axis, [(source, source + steps) for source in range(l...  10 us
    dot_general x4, matrix products, on_device(): jnp.einsum('ltjab,ltjbs->ltas', explicit_tiles, picked, preferred_element...  6.59 us
  transfers between devices with their start and end apart: 20, of which 18 were waited for; matrix products, arithmetic and copies ran while one was open for 2% of the time, Pallas kernels for 0%

commit v1 on v0

--- a/solution.py
+++ b/solution.py
@@ -54,7 +54,12 @@
     source = surface_source.astype(jnp.float32)
     fall_rate = settling[None, None, :]
     wet_cells = wet_mask.astype(jnp.bfloat16)[:, :, None]
-    all_columns = lax.all_gather(implicit_columns, "vert", axis=0, tiled=True)
+    ring = [implicit_columns]
+    for hop in range(3):
+        ring.append(lax.ppermute(ring[-1], "vert", [(dev, (dev + 1) % 4) for dev in range(4)]))
+    all_columns = jnp.roll(
+        jnp.concatenate(ring[::-1], axis=0), (lax.axis_index("vert") + 1) * ring[0].shape[0], axis=0
+    )
     own_rows = lax.dynamic_slice_in_dim(all_columns, first_level, lev_dev, 1)
     current = tracer
     for step_index in range(STEPS):

time: 169 us -> 160 us (0.947)
  blocking collectives: 44.9 us -> 33.4 us
  starting transfers between devices: 55.3 us -> 61 us
  local copies, waits for them, and re-layouts: 9.57 us -> 6.21 us
  matrix products: 11.4 us -> 8.66 us
  other arithmetic: 5.1 us -> 7.45 us
    all_gather x1 -> x0, blocking collectives: 11.3 us -> none  [on_device(): all_columns = lax.all_gather(implicit_columns, 'vert', axis=0, tiled=True)]
    ppermute x0 -> x3, starting transfers between devices: none -> 5.45 us  [on_device(): lax.ppermute(ring[-1], 'vert', [(dev, (dev + 1) % 4) for dev in range(4)])]
    ppermute x0 -> x3, waiting for transfers between devices: none -> 3.99 us  [on_device(): lax.ppermute(ring[-1], 'vert', [(dev, (dev + 1) % 4) for dev in range(4)])]
    gather x4, local copies, waits for them, and re-layouts: 6.5 us -> 2.89 us  [on_device(): picked = flattened[position] * live_slots[:, :, :, None, None]]
    ppermute x8, waiting for transfers between devices: 25.3 us -> 21.9 us  [extended(): after = lax.ppermute(leading, axis, down)]
    dot_general x4, matrix products: 6.59 us -> 3.93 us  [on_device(): jnp.einsum('ltjab,ltjbs->ltas', explicit_tiles, picked, preferred_element...]
  transfers between devices with their start and end apart: 20 -> 23, of which waited for: 18 -> 19; matrix products, arithmetic and copies ran while one was open for 2% -> 4% of each run, Pallas kernels for 0% -> 0%
where the time goes in v1:
time: 160 us; the launch traced here: 159 us
  starting transfers between devices  61 us (38%)
  waiting for transfers between devices  41.4 us (26%)
  blocking collectives  33.4 us (21%)
  matrix products  8.66 us (5%)
  other arithmetic  7.45 us (5%)
  local copies, waits for them, and re-layouts  6.21 us (4%)
    all_gather x4, blocking collectives, on_device(): lax.all_gather(loaded, 'vert', axis=0, tiled=True).astype(jnp.float32)  33.4 us
    ppermute x8, starting transfers between devices, extended(): before = lax.ppermute(last, axis, up)  30.2 us
    ppermute x8, waiting for transfers between devices, extended(): after = lax.ppermute(leading, axis, down)  21.9 us
    ppermute x8, starting transfers between devices, extended(): after = lax.ppermute(leading, axis, down)  15.3 us
    ppermute x8, waiting for transfers between devices, extended(): before = lax.ppermute(last, axis, up)  10.8 us
    ppermute x4, starting transfers between devices, from_behind(): lax.ppermute(value, axis, [(source, source + steps) for source in range(l...  10 us
    ppermute x3, starting transfers between devices, on_device(): lax.ppermute(ring[-1], 'vert', [(dev, (dev + 1) % 4) for dev in range(4)])  5.45 us
    dot_general x4, matrix products, on_device(): jnp.einsum('ckm,mcs->kcs', own_rows, lax.all_gather(loaded, 'vert', axis=...  4.73 us
  transfers between devices with their start and end apart: 23, of which 19 were waited for; matrix products, arithmetic and copies ran while one was open for 4% of the time, Pallas kernels for 0%

profile of v1, /device:TPU:1, one launch (start us, length us, event | category | flops | bytes accessed | tf_op | source)
XLA Modules:
  0.0 158.7 jit_solution(13862008895483428939)
XLA Ops:
  0.0 1.4 collective-permute-start.1
  1.4 4.6 %collective-permute-start = (bf16[2,2,128,128]{3,2,1,0:T(8,128)(2,1)}, bf16[2,2,128,128]{3,2,1,0:T(8,128)(2,1)S(1)}, u32[]{:S(2)}, u32[]{:S(2)}) collective-permute-start(bf16[2,2,128,128]{3,2,1,0:T(8,128)(2,1)} %bitcast.87), channel_id=1, source_target_pairs={{0,4},{4,8},{8,12},{12,16},{16,20},{20,24},{24,28},{1,5},{5,9},{9,... | collective-permute-start | bytes 393224 | tf_op jit(solution)/shard_map/ppermute | solution.py:17
  6.0 2.6 %collective-permute-start.4 = (f32[64,8,8]{0,2,1:T(8,128)}, f32[64,8,8]{0,2,1:T(8,128)S(1)}, u32[]{:S(2)}, u32[]{:S(2)}) collective-permute-start(f32[64,8,8]{0,2,1:T(8,128)} %param.13), channel_id=1, source_target_pairs={{0,1},{1,2},{2,3},{3,0},{4,5},{5,6},{6,7},{7,4},{8,9},{9,10},{10,1... | collective-permute-start | bytes 49160 | tf_op jit(solution)/shard_map/ppermute | solution.py:59
  10.0 1.3 collective-permute-done
  12.3 2.4 %collective-permute-start.3 = (bf16[2,6,128,128]{3,2,1,0:T(8,128)(2,1)S(1)}, bf16[2,6,128,128]{3,2,1,0:T(8,128)(2,1)S(1)}, u32[]{:S(2)}, u32[]{:S(2)}) collective-permute-start(bf16[2,6,128,128]{3,2,1,0:T(8,128)(2,1)S(1)} %pad_maximum_fusion.4), channel_id=1, source_target_pairs={{1,0},{2,1},{3,2},{5,4},{6,5},{7,6},{9,8},{10,9},{11,10},{13,12},{... | collective-permute-start | bytes 1179656 | tf_op jit(solution)/shard_map/ppermute | solution.py:18
  14.7 3.2 %collective-permute-start.2 = (bf16[2,6,128,128]{3,2,1,0:T(8,128)(2,1)S(1)}, bf16[2,6,128,128]{3,2,1,0:T(8,128)(2,1)}, u32[]{:S(2)}, u32[]{:S(2)}) collective-permute-start(bf16[2,6,128,128]{3,2,1,0:T(8,128)(2,1)S(1)} %pad_maximum_fusion.4), channel_id=1, source_target_pairs={{0,1},{1,2},{2,3},{4,5},{5,6},{6,7},{8,9},{9,10},{10,11},{12,13},{... | collective-permute-start | bytes 1179656 | tf_op jit(solution)/shard_map/ppermute | solution.py:17
  19.1 3.8 %collective-permute-done.5 = f32[64,8,8]{0,2,1:T(8,128)S(1)} collective-permute-done((f32[64,8,8]{0,2,1:T(8,128)S(1)}, f32[64,8,8]{0,2,1:T(8,128)S(1)}, u32[]{:S(2)}, u32[]{:S(2)}) %collective-permute-start.5) | collective-permute-done | bytes 16416 | tf_op jit(solution)/shard_map/ppermute | solution.py:59
  22.9 2.5 %collective-permute-start.6 = (f32[64,8,8]{0,2,1:T(8,128)S(1)}, f32[64,8,8]{0,2,1:T(8,128)S(1)}, u32[]{:S(2)}, u32[]{:S(2)}) collective-permute-start(f32[64,8,8]{0,2,1:T(8,128)S(1)} %collective-permute-done.5), channel_id=1, source_target_pairs={{0,1},{1,2},{2,3},{3,0},{4,5},{5,6},{6,7},{7,4},{8,9},{9,10},{10,1... | collective-permute-start | bytes 49160 | tf_op jit(solution)/shard_map/ppermute | solution.py:59
  30.1 8.2 %all_gather.12 = bf16[8,256,128]{2,1,0:T(8,128)(2,1)S(1)} all-gather(bf16[2,256,128]{2,1,0:T(8,128)(2,1)S(1)} %fusion.16), channel_id=1, replica_groups=mesh['horiz'=8,'vert'=4] {'vert'}, dimensions={0}, use_global_device_ids=true | all-gather | bytes 655360 | tf_op jit(solution)/shard_map/all_gather | solution.py:79
  38.4 1.2 convolution_bitcast_fusion.3
  39.7 2.5 %collective-permute-start.7 = (bf16[256,128]{1,0:T(8,128)(2,1)S(1)}, bf16[256,128]{1,0:T(8,128)(2,1)S(1)}, u32[]{:S(2)}, u32[]{:S(2)}) collective-permute-start(bf16[256,128]{1,0:T(8,128)(2,1)S(1)} %bitcast.94), channel_id=1, source_target_pairs={{0,1},{1,2},{2,3},{4,5},{5,6},{6,7},{8,9},{9,10},{10,11},{12,13},{... | collective-permute-start | bytes 196616 | tf_op jit(solution)/shard_map/ppermute | solution.py:26
  44.0 4.0 %collective-permute-start.8 = (bf16[2,2,128,128]{3,2,1,0:T(8,128)(2,1)S(1)}, bf16[2,2,128,128]{3,2,1,0:T(8,128)(2,1)S(1)}, u32[]{:S(2)}, u32[]{:S(2)}) collective-permute-start(bf16[2,2,128,128]{3,2,1,0:T(8,128)(2,1)S(1)} %copy.46), channel_id=1, source_target_pairs={{0,4},{4,8},{8,12},{12,16},{16,20},{20,24},{24,28},{1,5},{5,9},{9,... | collective-permute-start | bytes 393224 | tf_op jit(solution)/shard_map/ppermute | solution.py:17
  48.0 1.3 collective-permute-start.9
  49.3 2.0 %collective-permute-done.8 = bf16[2,2,128,128]{3,2,1,0:T(8,128)(2,1)S(1)} collective-permute-done((bf16[2,2,128,128]{3,2,1,0:T(8,128)(2,1)S(1)}, bf16[2,2,128,128]{3,2,1,0:T(8,128)(2,1)S(1)}, u32[]{:S(2)}, u32[]{:S(2)}) %collective-permute-start.8) | collective-permute-done | bytes 131104 | tf_op jit(solution)/shard_map/ppermute | solution.py:17
  51.3 3.8 %collective-permute-done.9 = bf16[2,2,128,128]{3,2,1,0:T(8,128)(2,1)S(1)} collective-permute-done((bf16[2,2,128,128]{3,2,1,0:T(8,128)(2,1)S(1)}, bf16[2,2,128,128]{3,2,1,0:T(8,128)(2,1)S(1)}, u32[]{:S(2)}, u32[]{:S(2)}) %collective-permute-start.9) | collective-permute-done | bytes 131104 | tf_op jit(solution)/shard_map/ppermute | solution.py:18
  55.2 2.5 %collective-permute-start.11 = (bf16[2,6,128,128]{3,2,1,0:T(8,128)(2,1)S(1)}, bf16[2,6,128,128]{3,2,1,0:T(8,128)(2,1)S(1)}, u32[]{:S(2)}, u32[]{:S(2)}) collective-permute-start(bf16[2,6,128,128]{3,2,1,0:T(8,128)(2,1)S(1)} %constant_dynamic-update-slice_fusion), channel_id=1, source_target_pairs={{1,0},{2,1},{3,2},{5,4},{6,5},{7,6},{9,8},{10,9},{11,10},{13,12},{... | collective-permute-start | bytes 1179656 | tf_op jit(solution)/shard_map/ppermute | solution.py:18
  57.7 3.6 %collective-permute-start.10 = (bf16[2,6,128,128]{3,2,1,0:T(8,128)(2,1)S(1)}, bf16[2,6,128,128]{3,2,1,0:T(8,128)(2,1)S(1)}, u32[]{:S(2)}, u32[]{:S(2)}) collective-permute-start(bf16[2,6,128,128]{3,2,1,0:T(8,128)(2,1)S(1)} %constant_dynamic-update-slice_fusion), channel_id=1, source_target_pairs={{0,1},{1,2},{2,3},{4,5},{5,6},{6,7},{8,9},{9,10},{10,11},{12,13},{... | collective-permute-start | bytes 1179656 | tf_op jit(solution)/shard_map/ppermute | solution.py:17
  61.4 3.5 %collective-permute-done.11 = bf16[2,6,128,128]{3,2,1,0:T(8,128)(2,1)S(1)} collective-permute-done((bf16[2,6,128,128]{3,2,1,0:T(8,128)(2,1)S(1)}, bf16[2,6,128,128]{3,2,1,0:T(8,128)(2,1)S(1)}, u32[]{:S(2)}, u32[]{:S(2)}) %collective-permute-start.11) | collective-permute-done | bytes 393248 | tf_op jit(solution)/shard_map/ppermute | solution.py:18
  64.9 1.2 collective-permute-done.10
  68.2 8.4 %all_gather.13 = bf16[8,256,128]{2,1,0:T(8,128)(2,1)S(1)} all-gather(bf16[2,256,128]{2,1,0:T(8,128)(2,1)S(1)} %fusion.17), channel_id=1, replica_groups=mesh['horiz'=8,'vert'=4] {'vert'}, dimensions={0}, use_global_device_ids=true | all-gather | bytes 655360 | tf_op jit(solution)/shard_map/all_gather | solution.py:79
  76.6 1.2 convolution_bitcast_fusion.2
  77.9 2.5 %collective-permute-start.12 = (bf16[256,128]{1,0:T(8,128)(2,1)S(1)}, bf16[256,128]{1,0:T(8,128)(2,1)S(1)}, u32[]{:S(2)}, u32[]{:S(2)}) collective-permute-start(bf16[256,128]{1,0:T(8,128)(2,1)S(1)} %bitcast.95), channel_id=1, source_target_pairs={{0,1},{1,2},{2,3},{4,5},{5,6},{6,7},{8,9},{9,10},{10,11},{12,13},{... | collective-permute-start | bytes 196616 | tf_op jit(solution)/shard_map/ppermute | solution.py:26
  80.5 1.2 collective-permute-done.12
  82.2 4.2 %collective-permute-start.13 = (bf16[2,2,128,128]{3,2,1,0:T(8,128)(2,1)S(1)}, bf16[2,2,128,128]{3,2,1,0:T(8,128)(2,1)S(1)}, u32[]{:S(2)}, u32[]{:S(2)}) collective-permute-start(bf16[2,2,128,128]{3,2,1,0:T(8,128)(2,1)S(1)} %copy.51), channel_id=1, source_target_pairs={{0,4},{4,8},{8,12},{12,16},{16,20},{20,24},{24,28},{1,5},{5,9},{9,... | collective-permute-start | bytes 393224 | tf_op jit(solution)/shard_map/ppermute | solution.py:17
  86.3 1.3 collective-permute-start.14
  87.6 2.0 %collective-permute-done.13 = bf16[2,2,128,128]{3,2,1,0:T(8,128)(2,1)S(1)} collective-permute-done((bf16[2,2,128,128]{3,2,1,0:T(8,128)(2,1)S(1)}, bf16[2,2,128,128]{3,2,1,0:T(8,128)(2,1)S(1)}, u32[]{:S(2)}, u32[]{:S(2)}) %collective-permute-start.13) | collective-permute-done | bytes 131104 | tf_op jit(solution)/shard_map/ppermute | solution.py:17
  89.7 3.8 %collective-permute-done.14 = bf16[2,2,128,128]{3,2,1,0:T(8,128)(2,1)S(1)} collective-permute-done((bf16[2,2,128,128]{3,2,1,0:T(8,128)(2,1)S(1)}, bf16[2,2,128,128]{3,2,1,0:T(8,128)(2,1)S(1)}, u32[]{:S(2)}, u32[]{:S(2)}) %collective-permute-start.14) | collective-permute-done | bytes 131104 | tf_op jit(solution)/shard_map/ppermute | solution.py:18
  93.5 2.5 %collective-permute-start.16 = (bf16[2,6,128,128]{3,2,1,0:T(8,128)(2,1)S(1)}, bf16[2,6,128,128]{3,2,1,0:T(8,128)(2,1)S(1)}, u32[]{:S(2)}, u32[]{:S(2)}) collective-permute-start(bf16[2,6,128,128]{3,2,1,0:T(8,128)(2,1)S(1)} %constant_dynamic-update-slice_fusion.3), channel_id=1, source_target_pairs={{1,0},{2,1},{3,2},{5,4},{6,5},{7,6},{9,8},{10,9},{11,10},{13,12},{... | collective-permute-start | bytes 1179656 | tf_op jit(solution)/shard_map/ppermute | solution.py:18
  96.1 3.6 %collective-permute-start.15 = (bf16[2,6,128,128]{3,2,1,0:T(8,128)(2,1)S(1)}, bf16[2,6,128,128]{3,2,1,0:T(8,128)(2,1)S(1)}, u32[]{:S(2)}, u32[]{:S(2)}) collective-permute-start(bf16[2,6,128,128]{3,2,1,0:T(8,128)(2,1)S(1)} %constant_dynamic-update-slice_fusion.3), channel_id=1, source_target_pairs={{0,1},{1,2},{2,3},{4,5},{5,6},{6,7},{8,9},{9,10},{10,11},{12,13},{... | collective-permute-start | bytes 1179656 | tf_op jit(solution)/shard_map/ppermute | solution.py:17
  99.7 3.5 %collective-permute-done.16 = bf16[2,6,128,128]{3,2,1,0:T(8,128)(2,1)S(1)} collective-permute-done((bf16[2,6,128,128]{3,2,1,0:T(8,128)(2,1)S(1)}, bf16[2,6,128,128]{3,2,1,0:T(8,128)(2,1)S(1)}, u32[]{:S(2)}, u32[]{:S(2)}) %collective-permute-start.16) | collective-permute-done | bytes 393248 | tf_op jit(solution)/shard_map/ppermute | solution.py:18
  103.2 1.2 collective-permute-done.15
  106.5 8.4 %all_gather.14 = bf16[8,256,128]{2,1,0:T(8,128)(2,1)S(1)} all-gather(bf16[2,256,128]{2,1,0:T(8,128)(2,1)S(1)} %fusion.18), channel_id=1, replica_groups=mesh['horiz'=8,'vert'=4] {'vert'}, dimensions={0}, use_global_device_ids=true | all-gather | bytes 655360 | tf_op jit(solution)/shard_map/all_gather | solution.py:79
  114.9 1.2 convolution_bitcast_fusion.1
  116.3 2.5 %collective-permute-start.17 = (bf16[256,128]{1,0:T(8,128)(2,1)S(1)}, bf16[256,128]{1,0:T(8,128)(2,1)S(1)}, u32[]{:S(2)}, u32[]{:S(2)}) collective-permute-start(bf16[256,128]{1,0:T(8,128)(2,1)S(1)} %bitcast.96), channel_id=1, source_target_pairs={{0,1},{1,2},{2,3},{4,5},{5,6},{6,7},{8,9},{9,10},{10,11},{12,13},{... | collective-permute-start | bytes 196616 | tf_op jit(solution)/shard_map/ppermute | solution.py:26
  118.9 1.2 collective-permute-done.17
  120.5 3.3 %collective-permute-start.18 = (bf16[2,2,128,128]{3,2,1,0:T(8,128)(2,1)S(1)}, bf16[2,2,128,128]{3,2,1,0:T(8,128)(2,1)S(1)}, u32[]{:S(2)}, u32[]{:S(2)}) collective-permute-start(bf16[2,2,128,128]{3,2,1,0:T(8,128)(2,1)S(1)} %copy.55), channel_id=1, source_target_pairs={{0,4},{4,8},{8,12},{12,16},{16,20},{20,24},{24,28},{1,5},{5,9},{9,... | collective-permute-start | bytes 393224 | tf_op jit(solution)/shard_map/ppermute | solution.py:17
  123.8 1.3 collective-permute-start.19
  125.1 2.0 %collective-permute-done.18 = bf16[2,2,128,128]{3,2,1,0:T(8,128)(2,1)S(1)} collective-permute-done((bf16[2,2,128,128]{3,2,1,0:T(8,128)(2,1)S(1)}, bf16[2,2,128,128]{3,2,1,0:T(8,128)(2,1)S(1)}, u32[]{:S(2)}, u32[]{:S(2)}) %collective-permute-start.18) | collective-permute-done | bytes 131104 | tf_op jit(solution)/shard_map/ppermute | solution.py:17
  127.2 3.8 %collective-permute-done.19 = bf16[2,2,128,128]{3,2,1,0:T(8,128)(2,1)S(1)} collective-permute-done((bf16[2,2,128,128]{3,2,1,0:T(8,128)(2,1)S(1)}, bf16[2,2,128,128]{3,2,1,0:T(8,128)(2,1)S(1)}, u32[]{:S(2)}, u32[]{:S(2)}) %collective-permute-start.19) | collective-permute-done | bytes 131104 | tf_op jit(solution)/shard_map/ppermute | solution.py:18
  131.0 2.5 %collective-permute-start.21 = (bf16[2,6,128,128]{3,2,1,0:T(8,128)(2,1)S(1)}, bf16[2,6,128,128]{3,2,1,0:T(8,128)(2,1)S(1)}, u32[]{:S(2)}, u32[]{:S(2)}) collective-permute-start(bf16[2,6,128,128]{3,2,1,0:T(8,128)(2,1)S(1)} %constant_dynamic-update-slice_fusion.6), channel_id=1, source_target_pairs={{1,0},{2,1},{3,2},{5,4},{6,5},{7,6},{9,8},{10,9},{11,10},{13,12},{... | collective-permute-start | bytes 1179656 | tf_op jit(solution)/shard_map/ppermute | solution.py:18
  133.6 3.8 %collective-permute-start.20 = (bf16[2,6,128,128]{3,2,1,0:T(8,128)(2,1)S(1)}, bf16[2,6,128,128]{3,2,1,0:T(8,128)(2,1)S(1)}, u32[]{:S(2)}, u32[]{:S(2)}) collective-permute-start(bf16[2,6,128,128]{3,2,1,0:T(8,128)(2,1)S(1)} %constant_dynamic-update-slice_fusion.6), channel_id=1, source_target_pairs={{0,1},{1,2},{2,3},{4,5},{5,6},{6,7},{8,9},{9,10},{10,11},{12,13},{... | collective-permute-start | bytes 1179656 | tf_op jit(solution)/shard_map/ppermute | solution.py:17
  137.4 3.3 %collective-permute-done.21 = bf16[2,6,128,128]{3,2,1,0:T(8,128)(2,1)S(1)} collective-permute-done((bf16[2,6,128,128]{3,2,1,0:T(8,128)(2,1)S(1)}, bf16[2,6,128,128]{3,2,1,0:T(8,128)(2,1)S(1)}, u32[]{:S(2)}, u32[]{:S(2)}) %collective-permute-start.21) | collective-permute-done | bytes 393248 | tf_op jit(solution)/shard_map/ppermute | solution.py:18
  140.7 1.2 collective-permute-done.20
  142.7 1.2 fusion
  144.0 8.4 %all_gather.15 = bf16[8,256,128]{2,1,0:T(8,128)(2,1)S(1)} all-gather(bf16[2,256,128]{2,1,0:T(8,128)(2,1)S(1)} %fusion.19), channel_id=1, replica_groups=mesh['horiz'=8,'vert'=4] {'vert'}, dimensions={0}, use_global_device_ids=true | all-gather | bytes 655360 | tf_op jit(solution)/shard_map/all_gather | solution.py:79
  152.4 1.2 convolution_bitcast_fusion
  153.8 2.5 %collective-permute-start.22 = (bf16[256,128]{1,0:T(8,128)(2,1)S(1)}, bf16[256,128]{1,0:T(8,128)(2,1)S(1)}, u32[]{:S(2)}, u32[]{:S(2)}) collective-permute-start(bf16[256,128]{1,0:T(8,128)(2,1)S(1)} %bitcast.97), channel_id=1, source_target_pairs={{0,1},{1,2},{2,3},{4,5},{5,6},{6,7},{8,9},{9,10},{10,11},{12,13},{... | collective-permute-start | bytes 196616 | tf_op jit(solution)/shard_map/ppermute | solution.py:26
  156.4 1.2 collective-permute-done.22
  (76 shorter events, 18.0 us)
Async XLA Ops:
  0.0 29.5 %copy-start = (bf16[2,2,7,128,128]{4,3,2,1,0:T(8,128)(2,1)S(1)}, bf16[2,2,7,128,128]{4,3,2,1,0:T(8,128)(2,1)}, u32[]{:S(2)}) copy-start(bf16[2,2,7,128,128]{4,3,2,1,0:T(8,128)(2,1)} %param.9) | copy-start | bytes 2752516
  0.0 27.6 %copy-start.1 = (bf16[2,256,128]{2,1,0:T(8,128)(2,1)S(1)}, bf16[2,256,128]{2,1,0:T(8,128)(2,1)}, u32[]{:S(2)}) copy-start(bf16[2,256,128]{2,1,0:T(8,128)(2,1)} %param.8) | copy-start | bytes 393220
  0.0 10.0 %collective-permute-start.1 = (bf16[2,2,128,128]{3,2,1,0:T(8,128)(2,1)}, bf16[2,2,128,128]{3,2,1,0:T(8,128)(2,1)S(1)}, u32[]{:S(2)}, u32[]{:S(2)}) collective-permute-start(bf16[2,2,128,128]{3,2,1,0:T(8,128)(2,1)} %bitcast.86), channel_id=1, source_target_pairs={{4,0},{8,4},{12,8},{16,12},{20,16},{24,20},{28,24},{5,1},{9,5},{13... | collective-permute-start | bytes 393224 | tf_op jit(solution)/shard_map/ppermute | solution.py:18
  1.4 9.9 %collective-permute-start = (bf16[2,2,128,128]{3,2,1,0:T(8,128)(2,1)}, bf16[2,2,128,128]{3,2,1,0:T(8,128)(2,1)S(1)}, u32[]{:S(2)}, u32[]{:S(2)}) collective-permute-start(bf16[2,2,128,128]{3,2,1,0:T(8,128)(2,1)} %bitcast.87), channel_id=1, source_target_pairs={{0,4},{4,8},{8,12},{12,16},{16,20},{20,24},{24,28},{1,5},{5,9},{9,... | collective-permute-start | bytes 393224 | tf_op jit(solution)/shard_map/ppermute | solution.py:17
  6.0 12.7 %collective-permute-start.4 = (f32[64,8,8]{0,2,1:T(8,128)}, f32[64,8,8]{0,2,1:T(8,128)S(1)}, u32[]{:S(2)}, u32[]{:S(2)}) collective-permute-start(f32[64,8,8]{0,2,1:T(8,128)} %param.13), channel_id=1, source_target_pairs={{0,1},{1,2},{2,3},{3,0},{4,5},{5,6},{6,7},{7,4},{8,9},{9,10},{10,1... | collective-permute-start | bytes 49160 | tf_op jit(solution)/shard_map/ppermute | solution.py:59
  12.3 15.3 %collective-permute-start.3 = (bf16[2,6,128,128]{3,2,1,0:T(8,128)(2,1)S(1)}, bf16[2,6,128,128]{3,2,1,0:T(8,128)(2,1)S(1)}, u32[]{:S(2)}, u32[]{:S(2)}) collective-permute-start(bf16[2,6,128,128]{3,2,1,0:T(8,128)(2,1)S(1)} %pad_maximum_fusion.4), channel_id=1, source_target_pairs={{1,0},{2,1},{3,2},{5,4},{6,5},{7,6},{9,8},{10,9},{11,10},{13,12},{... | collective-permute-start | bytes 1179656 | tf_op jit(solution)/shard_map/ppermute | solution.py:18
  14.7 12.9 %collective-permute-start.2 = (bf16[2,6,128,128]{3,2,1,0:T(8,128)(2,1)S(1)}, bf16[2,6,128,128]{3,2,1,0:T(8,128)(2,1)}, u32[]{:S(2)}, u32[]{:S(2)}) collective-permute-start(bf16[2,6,128,128]{3,2,1,0:T(8,128)(2,1)S(1)} %pad_maximum_fusion.4), channel_id=1, source_target_pairs={{0,1},{1,2},{2,3},{4,5},{5,6},{6,7},{8,9},{9,10},{10,11},{12,13},{... | collective-permute-start | bytes 1179656 | tf_op jit(solution)/shard_map/ppermute | solution.py:17
  18.6 11.4 %copy-start.3 = (bf16[2,2,7]{2,1,0:T(2,128)(2,1)}, bf16[2,2,7]{2,1,0:T(2,128)(2,1)S(1)}, u32[]{:S(2)}) copy-start(bf16[2,2,7]{2,1,0:T(2,128)(2,1)S(1)} %compare_convert_fusion) | copy-start | bytes 172
  18.7 4.2 %collective-permute-start.5 = (f32[64,8,8]{0,2,1:T(8,128)S(1)}, f32[64,8,8]{0,2,1:T(8,128)S(1)}, u32[]{:S(2)}, u32[]{:S(2)}) collective-permute-start(f32[64,8,8]{0,2,1:T(8,128)S(1)} %collective-permute-done.4), channel_id=1, source_target_pairs={{0,1},{1,2},{2,3},{3,0},{4,5},{5,6},{6,7},{7,4},{8,9},{9,10},{10,1... | collective-permute-start | bytes 49160 | tf_op jit(solution)/shard_map/ppermute | solution.py:59
  22.9 3.5 %collective-permute-start.6 = (f32[64,8,8]{0,2,1:T(8,128)S(1)}, f32[64,8,8]{0,2,1:T(8,128)S(1)}, u32[]{:S(2)}, u32[]{:S(2)}) collective-permute-start(f32[64,8,8]{0,2,1:T(8,128)S(1)} %collective-permute-done.5), channel_id=1, source_target_pairs={{0,1},{1,2},{2,3},{3,0},{4,5},{5,6},{6,7},{7,4},{8,9},{9,10},{10,1... | collective-permute-start | bytes 49160 | tf_op jit(solution)/shard_map/ppermute | solution.py:59
  30.1 12.1 %copy-start.2 = (f32[128]{0:T(128)S(1)}, f32[128]{0:T(128)}, u32[]{:S(2)}) copy-start(f32[128]{0:T(128)} %param.14) | copy-start | bytes 1540
  39.7 3.8 %collective-permute-start.7 = (bf16[256,128]{1,0:T(8,128)(2,1)S(1)}, bf16[256,128]{1,0:T(8,128)(2,1)S(1)}, u32[]{:S(2)}, u32[]{:S(2)}) collective-permute-start(bf16[256,128]{1,0:T(8,128)(2,1)S(1)} %bitcast.94), channel_id=1, source_target_pairs={{0,1},{1,2},{2,3},{4,5},{5,6},{6,7},{8,9},{9,10},{10,11},{12,13},{... | collective-permute-start | bytes 196616 | tf_op jit(solution)/shard_map/ppermute | solution.py:26
  44.0 7.3 %collective-permute-start.8 = (bf16[2,2,128,128]{3,2,1,0:T(8,128)(2,1)S(1)}, bf16[2,2,128,128]{3,2,1,0:T(8,128)(2,1)S(1)}, u32[]{:S(2)}, u32[]{:S(2)}) collective-permute-start(bf16[2,2,128,128]{3,2,1,0:T(8,128)(2,1)S(1)} %copy.46), channel_id=1, source_target_pairs={{0,4},{4,8},{8,12},{12,16},{16,20},{20,24},{24,28},{1,5},{5,9},{9,... | collective-permute-start | bytes 393224 | tf_op jit(solution)/shard_map/ppermute | solution.py:17
  48.0 7.2 %collective-permute-start.9 = (bf16[2,2,128,128]{3,2,1,0:T(8,128)(2,1)S(1)}, bf16[2,2,128,128]{3,2,1,0:T(8,128)(2,1)S(1)}, u32[]{:S(2)}, u32[]{:S(2)}) collective-permute-start(bf16[2,2,128,128]{3,2,1,0:T(8,128)(2,1)S(1)} %copy.46), channel_id=1, source_target_pairs={{4,0},{8,4},{12,8},{16,12},{20,16},{24,20},{28,24},{5,1},{9,5},{13... | collective-permute-start | bytes 393224 | tf_op jit(solution)/shard_map/ppermute | solution.py:18
  55.2 9.7 %collective-permute-start.11 = (bf16[2,6,128,128]{3,2,1,0:T(8,128)(2,1)S(1)}, bf16[2,6,128,128]{3,2,1,0:T(8,128)(2,1)S(1)}, u32[]{:S(2)}, u32[]{:S(2)}) collective-permute-start(bf16[2,6,128,128]{3,2,1,0:T(8,128)(2,1)S(1)} %constant_dynamic-update-slice_fusion), channel_id=1, source_target_pairs={{1,0},{2,1},{3,2},{5,4},{6,5},{7,6},{9,8},{10,9},{11,10},{13,12},{... | collective-permute-start | bytes 1179656 | tf_op jit(solution)/shard_map/ppermute | solution.py:18
  57.7 8.3 %collective-permute-start.10 = (bf16[2,6,128,128]{3,2,1,0:T(8,128)(2,1)S(1)}, bf16[2,6,128,128]{3,2,1,0:T(8,128)(2,1)S(1)}, u32[]{:S(2)}, u32[]{:S(2)}) collective-permute-start(bf16[2,6,128,128]{3,2,1,0:T(8,128)(2,1)S(1)} %constant_dynamic-update-slice_fusion), channel_id=1, source_target_pairs={{0,1},{1,2},{2,3},{4,5},{5,6},{6,7},{8,9},{9,10},{10,11},{12,13},{... | collective-permute-start | bytes 1179656 | tf_op jit(solution)/shard_map/ppermute | solution.py:17
  77.9 3.8 %collective-permute-start.12 = (bf16[256,128]{1,0:T(8,128)(2,1)S(1)}, bf16[256,128]{1,0:T(8,128)(2,1)S(1)}, u32[]{:S(2)}, u32[]{:S(2)}) collective-permute-start(bf16[256,128]{1,0:T(8,128)(2,1)S(1)} %bitcast.95), channel_id=1, source_target_pairs={{0,1},{1,2},{2,3},{4,5},{5,6},{6,7},{8,9},{9,10},{10,11},{12,13},{... | collective-permute-start | bytes 196616 | tf_op jit(solution)/shard_map/ppermute | solution.py:26
  82.2 7.4 %collective-permute-start.13 = (bf16[2,2,128,128]{3,2,1,0:T(8,128)(2,1)S(1)}, bf16[2,2,128,128]{3,2,1,0:T(8,128)(2,1)S(1)}, u32[]{:S(2)}, u32[]{:S(2)}) collective-permute-start(bf16[2,2,128,128]{3,2,1,0:T(8,128)(2,1)S(1)} %copy.51), channel_id=1, source_target_pairs={{0,4},{4,8},{8,12},{12,16},{16,20},{20,24},{24,28},{1,5},{5,9},{9,... | collective-permute-start | bytes 393224 | tf_op jit(solution)/shard_map/ppermute | solution.py:17
  86.3 7.2 %collective-permute-start.14 = (bf16[2,2,128,128]{3,2,1,0:T(8,128)(2,1)S(1)}, bf16[2,2,128,128]{3,2,1,0:T(8,128)(2,1)S(1)}, u32[]{:S(2)}, u32[]{:S(2)}) collective-permute-start(bf16[2,2,128,128]{3,2,1,0:T(8,128)(2,1)S(1)} %copy.51), channel_id=1, source_target_pairs={{4,0},{8,4},{12,8},{16,12},{20,16},{24,20},{28,24},{5,1},{9,5},{13... | collective-permute-start | bytes 393224 | tf_op jit(solution)/shard_map/ppermute | solution.py:18
  93.5 9.7 %collective-permute-start.16 = (bf16[2,6,128,128]{3,2,1,0:T(8,128)(2,1)S(1)}, bf16[2,6,128,128]{3,2,1,0:T(8,128)(2,1)S(1)}, u32[]{:S(2)}, u32[]{:S(2)}) collective-permute-start(bf16[2,6,128,128]{3,2,1,0:T(8,128)(2,1)S(1)} %constant_dynamic-update-slice_fusion.3), channel_id=1, source_target_pairs={{1,0},{2,1},{3,2},{5,4},{6,5},{7,6},{9,8},{10,9},{11,10},{13,12},{... | collective-permute-start | bytes 1179656 | tf_op jit(solution)/shard_map/ppermute | solution.py:18
  96.1 8.3 %collective-permute-start.15 = (bf16[2,6,128,128]{3,2,1,0:T(8,128)(2,1)S(1)}, bf16[2,6,128,128]{3,2,1,0:T(8,128)(2,1)S(1)}, u32[]{:S(2)}, u32[]{:S(2)}) collective-permute-start(bf16[2,6,128,128]{3,2,1,0:T(8,128)(2,1)S(1)} %constant_dynamic-update-slice_fusion.3), channel_id=1, source_target_pairs={{0,1},{1,2},{2,3},{4,5},{5,6},{6,7},{8,9},{9,10},{10,11},{12,13},{... | collective-permute-start | bytes 1179656 | tf_op jit(solution)/shard_map/ppermute | solution.py:17
  116.3 3.8 %collective-permute-start.17 = (bf16[256,128]{1,0:T(8,128)(2,1)S(1)}, bf16[256,128]{1,0:T(8,128)(2,1)S(1)}, u32[]{:S(2)}, u32[]{:S(2)}) collective-permute-start(bf16[256,128]{1,0:T(8,128)(2,1)S(1)} %bitcast.96), channel_id=1, source_target_pairs={{0,1},{1,2},{2,3},{4,5},{5,6},{6,7},{8,9},{9,10},{10,11},{12,13},{... | collective-permute-start | bytes 196616 | tf_op jit(solution)/shard_map/ppermute | solution.py:26
  120.5 6.6 %collective-permute-start.18 = (bf16[2,2,128,128]{3,2,1,0:T(8,128)(2,1)S(1)}, bf16[2,2,128,128]{3,2,1,0:T(8,128)(2,1)S(1)}, u32[]{:S(2)}, u32[]{:S(2)}) collective-permute-start(bf16[2,2,128,128]{3,2,1,0:T(8,128)(2,1)S(1)} %copy.55), channel_id=1, source_target_pairs={{0,4},{4,8},{8,12},{12,16},{16,20},{20,24},{24,28},{1,5},{5,9},{9,... | collective-permute-start | bytes 393224 | tf_op jit(solution)/shard_map/ppermute | solution.py:17
  123.8 7.2 %collective-permute-start.19 = (bf16[2,2,128,128]{3,2,1,0:T(8,128)(2,1)S(1)}, bf16[2,2,128,128]{3,2,1,0:T(8,128)(2,1)S(1)}, u32[]{:S(2)}, u32[]{:S(2)}) collective-permute-start(bf16[2,2,128,128]{3,2,1,0:T(8,128)(2,1)S(1)} %copy.55), channel_id=1, source_target_pairs={{4,0},{8,4},{12,8},{16,12},{20,16},{24,20},{28,24},{5,1},{9,5},{13... | collective-permute-start | bytes 393224 | tf_op jit(solution)/shard_map/ppermute | solution.py:18
  131.0 9.7 %collective-permute-start.21 = (bf16[2,6,128,128]{3,2,1,0:T(8,128)(2,1)S(1)}, bf16[2,6,128,128]{3,2,1,0:T(8,128)(2,1)S(1)}, u32[]{:S(2)}, u32[]{:S(2)}) collective-permute-start(bf16[2,6,128,128]{3,2,1,0:T(8,128)(2,1)S(1)} %constant_dynamic-update-slice_fusion.6), channel_id=1, source_target_pairs={{1,0},{2,1},{3,2},{5,4},{6,5},{7,6},{9,8},{10,9},{11,10},{13,12},{... | collective-permute-start | bytes 1179656 | tf_op jit(solution)/shard_map/ppermute | solution.py:18
  133.6 8.3 %collective-permute-start.20 = (bf16[2,6,128,128]{3,2,1,0:T(8,128)(2,1)S(1)}, bf16[2,6,128,128]{3,2,1,0:T(8,128)(2,1)S(1)}, u32[]{:S(2)}, u32[]{:S(2)}) collective-permute-start(bf16[2,6,128,128]{3,2,1,0:T(8,128)(2,1)S(1)} %constant_dynamic-update-slice_fusion.6), channel_id=1, source_target_pairs={{0,1},{1,2},{2,3},{4,5},{5,6},{6,7},{8,9},{9,10},{10,11},{12,13},{... | collective-permute-start | bytes 1179656 | tf_op jit(solution)/shard_map/ppermute | solution.py:17
  153.8 3.8 %collective-permute-start.22 = (bf16[256,128]{1,0:T(8,128)(2,1)S(1)}, bf16[256,128]{1,0:T(8,128)(2,1)S(1)}, u32[]{:S(2)}, u32[]{:S(2)}) collective-permute-start(bf16[256,128]{1,0:T(8,128)(2,1)S(1)} %bitcast.97), channel_id=1, source_target_pairs={{0,1},{1,2},{2,3},{4,5},{5,6},{6,7},{8,9},{9,10},{10,11},{12,13},{... | collective-permute-start | bytes 196616 | tf_op jit(solution)/shard_map/ppermute | solution.py:26
